TPU v7x, 32 devices: a whole 2x2x4 slice. The times are simulated.
32 devices in a mesh: groups: 2 (over y), inst: 4 (over z), tp: 4 (over x, core).
Axes of the slice: x: 2, y: 2, z: 4, core: 2. Of those that a mesh axis runs over, the one named last changes fastest.
Arguments:
- key_value_pool: bfloat16 [272, 2, 8, 128, 128], P(('groups', 'inst'), None, 'tp'), parts along dimension 0, may hold values from -6 to 6
- key_value_scale: bfloat16 [272, 2, 8], P(('groups', 'inst'), None, 'tp'), parts along dimension 0, may hold values from 0.25 to 2
- lengths: int32 [64], P(('groups', 'inst')), parts along dimension 0, may hold values from 1 to 512, as said below
- table: int32 [64, 4], P(('groups', 'inst')), parts along dimension 0, may hold values from 0 to 33, as said below
- moves: int32 [16, 3], P('groups'), parts along dimension 0, may hold values from 0 to 33, as said below
- queries: bfloat16 [64, 4, 8192], P(('groups', 'inst'), None, 'tp'), parts along dimension 0, may hold values from -200 to 200
- new_kv: bfloat16 [64, 4, 2, 1024], P(('groups', 'inst'), None, None, 'tp'), parts along dimension 0, may hold values from -7 to 7
Outputs:
- attended: bfloat16 [64, 4, 8192], P(('groups', 'inst'), None, 'tp'), parts along dimension 0
- landed: bfloat16 [16, 2, 8, 128, 128], P(('groups', 'inst'), None, 'tp'), parts along dimension 0
- arrival_scales: bfloat16 [16, 2, 8], P(('groups', 'inst'), None, 'tp'), parts along dimension 0
- load: float32 [8], P(('groups', 'inst')), parts along dimension 0
There are 2 independent parts, one for each index of `groups`. A program takes and returns all parts, laid end to end along the dimension named above; each array names one. Nothing has to cross between parts.
Inputs may be any that keep to these rules, and one draw needn't show every extreme that they name: `lengths`: in every draw some slot that receives a migrated request holds 512 tokens. `table`: row b lists pool blocks of its own instance; block j holds tokens j * 128 to (j+1) * 128 - 1; the entries of one instance's rows are distinct; entries past a request's last block are not read. `moves`: row r: the source pool block holding the last block of the request leaving instance s = r // 2, its destination instance (s + 1 + r % 2) mod 4, and its destination slot; every instance receives 2 rows, with distinct slots; a source block is used by no table row of its instance.
All inputs are finite; a program needn't handle non-finite values.
Results may differ from a plain program's by a relative error of at most 0.0049.
Values may be sent and summed in bfloat16 or wider, within the bound.
A program may use at most 64 MiB of HBM per device.

v0:
```python
import math

import jax
import jax.numpy as jnp
from jax import lax
from jax.sharding import PartitionSpec as P


def softmax_parts(parts):
    masked = [jnp.where(allowed, scores, -1e30) for scores, allowed in parts]
    joined = jnp.concatenate(masked, axis=-1)
    highest = jnp.max(joined, axis=-1, keepdims=True)
    expsum = jnp.exp(joined - highest)
    weight_rows = (expsum / jnp.sum(expsum, axis=-1, keepdims=True)).astype(jnp.bfloat16)
    pieces = []
    offset = 0
    for scores, allowed in parts:
        width = scores.shape[-1]
        pieces.append(weight_rows[..., offset : offset + width])
        offset = offset + width
    return pieces


def local(key_value_pool, key_value_scale, lengths, table, moves, queries, new_kv):
    instances = lax.axis_size("inst")
    my_index = lax.axis_index("inst")
    slots = lengths.shape[0]
    per_source = moves.shape[0] // instances
    max_blocks = table.shape[1]
    heads = key_value_pool.shape[2]
    block_len = key_value_pool.shape[3]
    head_dim = key_value_pool.shape[4]
    steps = queries.shape[1]
    query_group = queries.shape[2] // (heads * head_dim)
    scaling = 1.0 / math.sqrt(head_dim)
    all_rows = jnp.arange(moves.shape[0], dtype=jnp.int32)
    targets = moves[:, 1]
    before = (targets[:, None] == targets[None, :]) & (all_rows[:, None] > all_rows[None, :])
    rank = jnp.sum(before.astype(jnp.int32), axis=1)
    ranks_here = jnp.arange(per_source, dtype=jnp.int32)
    arrival = (targets == my_index)[:, None] & (rank[:, None] == ranks_here[None, :])
    arrival_row = jnp.sum(jnp.where(arrival, all_rows[:, None], 0), axis=0)
    own_moves = lax.dynamic_slice_in_dim(moves, my_index * per_source, per_source, 0)
    leaving = jnp.take(key_value_pool, own_moves[:, 0], axis=0)
    leaving_scale = jnp.take(key_value_scale, own_moves[:, 0], axis=0)
    every_block, every_scale = (
        lax.all_gather(leaving, "inst", axis=0, tiled=True),
        lax.all_gather(leaving_scale, "inst", axis=0, tiled=True),
    )
    landed = jnp.take(every_block, arrival_row, axis=0)
    arrival_scales = jnp.take(every_scale, arrival_row, axis=0)
    tokens_here = jnp.sum((lengths + steps).astype(jnp.float32))
    total_tokens = lax.psum(tokens_here, "inst")
    load = (tokens_here * instances / total_tokens).reshape(1)
    arrival_slot = jnp.take(moves[:, 2], arrival_row)
    slot_ids = jnp.arange(slots, dtype=jnp.int32)
    slot_hit = slot_ids[:, None] == arrival_slot[None, :]
    incoming = jnp.any(slot_hit, axis=1)
    which_landed = jnp.sum(jnp.where(slot_hit, ranks_here[None, :], 0), axis=1)
    counts = (lengths + block_len - 1) // block_len
    block_ids = jnp.arange(max_blocks, dtype=jnp.int32)
    last_block = (block_ids[None, :] == counts[:, None] - 1) & incoming[:, None]
    flat_table = table.reshape(slots * max_blocks)
    cached = jnp.take(key_value_pool, flat_table, axis=0).reshape(
        slots, max_blocks, 2, heads, block_len, head_dim
    )
    cached_scale = (
        jnp.take(key_value_scale, flat_table, axis=0)
        .reshape(slots, max_blocks, 2, heads)
        .astype(jnp.float32)
    )
    arrived = jnp.take(landed, which_landed, axis=0)
    arrived_scale = jnp.take(arrival_scales, which_landed, axis=0).astype(jnp.float32)
    query_head_rows = queries.reshape(slots, steps, heads, query_group, head_dim)
    newest_keys = new_kv[:, :, 0].reshape(slots, steps, heads, head_dim)
    newest_values = new_kv[:, :, 1].reshape(slots, steps, heads, head_dim)
    positions = jnp.arange(max_blocks * block_len, dtype=jnp.int32)
    within = positions[None, :] < lengths[:, None]
    cached = jnp.where(last_block[:, :, None, None, None, None], arrived[:, None], cached)
    cached_scale = jnp.where(last_block[:, :, None, None], arrived_scale[:, None], cached_scale)
    key_scale = jnp.transpose(cached_scale[:, :, 0], (0, 2, 1))[:, None, :, None, :, None]
    cached_score_rows = jnp.einsum(
        "sthgd,sjhkd->sthgjk", query_head_rows, cached[:, :, 0], preferred_element_type=jnp.float32
    )
    cached_score_rows = (cached_score_rows * key_scale * scaling).reshape(
        slots, steps, heads, query_group, max_blocks * block_len
    )
    fresh_scores = (
        jnp.einsum(
            "sthgd,suhd->sthgu", query_head_rows, newest_keys, preferred_element_type=jnp.float32
        )
        * scaling
    )
    step_ids = jnp.arange(steps, dtype=jnp.int32)
    causal = (step_ids[None, :] <= step_ids[:, None])[None, :, None, None, :]
    parts = [(cached_score_rows, within[:, None, None, None, :])]
    parts.append((fresh_scores, causal))
    weight_rows = softmax_parts(parts)
    cached_weight_rows = weight_rows[0].reshape(
        slots, steps, heads, query_group, max_blocks, block_len
    )
    value_scale = jnp.transpose(cached_scale[:, :, 1], (0, 2, 1))[:, None, :, None, :, None]
    per_block = jnp.einsum(
        "sthgjk,sjhkd->sthgjd",
        cached_weight_rows,
        cached[:, :, 1],
        preferred_element_type=jnp.float32,
    )
    mixed = jnp.sum(per_block * value_scale, axis=4)
    mixed = mixed + jnp.einsum(
        "sthgu,suhd->sthgd", weight_rows[-1], newest_values, preferred_element_type=jnp.float32
    )
    attended = mixed.reshape(slots, steps, heads * query_group * head_dim).astype(jnp.bfloat16)
    return (attended, landed, arrival_scales, load)


def solution(mesh):
    placed = (
        P(("groups", "inst"), None, "tp", None, None),
        P(("groups", "inst"), None, "tp"),
        P(("groups", "inst")),
        P(("groups", "inst"), None),
        P("groups", None),
        P(("groups", "inst"), None, "tp"),
        P(("groups", "inst"), None, None, "tp"),
    )
    return jax.shard_map(
        local,
        mesh=mesh,
        in_specs=placed,
        out_specs=(
            P(("groups", "inst"), None, "tp"),
            P(("groups", "inst"), None, "tp", None, None),
            P(("groups", "inst"), None, "tp"),
            P(("groups", "inst")),
        ),
        check_vma=False,
    )
```

profile of v0, /device:TPU:0, one launch (start us, length us, event | category | flops | bytes accessed | tf_op | source)
XLA Modules:
  0.0 81.8 jit_solution(2833278176775155026)
XLA Ops:
  7.2 0.0 all-gather.2.cloned.1.call-start
  7.2 0.8 constant_dynamic-slice_fusion
  8.0 2.9 %gather_fusion.1 = bf16[2,2,2,128,128]{4,3,2,1,0:T(8,128)(2,1)S(1)} fusion(bf16[34,2,2,128,128]{4,3,2,1,0:T(8,128)(2,1)} %param.7, s32[1024]{0:T(1024)S(1)} %pad_clamp_fusion.2), kind=kCustom, calls=%fused_computation.1 | custom fusion | bytes 524296 | tf_op jit(solution)/shard_map/jit(_take)/gather | solution.py:44
  10.9 0.8 broadcast_select_fusion.1
  11.7 0.0 all-gather.2.cloned.1.call-update
  11.7 0.7 compare_bitcast_fusion
  12.4 0.8 slice_bitcast_fusion.15
  13.1 0.2 convert_reduce_fusion
  13.3 0.1 fusion.26
  13.5 0.6 gather_fusion
  14.1 0.1 select_reduce_fusion.1
  14.2 0.1 fusion.28
  14.3 0.7 fusion.32
  15.0 1.3 %convert_reduce_fusion.1 = f32[]{:T(128)} fusion(s32[8]{0:T(128)} %param.9), kind=kLoop, calls=%fused_computation.85 | loop fusion | flops 23 | bytes 36 | tf_op jit(solution)/shard_map/reduce_sum | solution.py:52
  16.2 0.8 copy.170
  17.0 0.6 gather_fusion.5
  17.6 0.1 broadcast_select_fusion.3
  17.7 0.7 compare_and_fusion
  18.4 0.8 copy.167
  19.1 12.7 %all_gather.7 = bf16[8,2,2]{2,1,0:T(2,128)(2,1)S(1)} all-gather(bf16[2,2,2]{2,1,0:T(2,128)(2,1)S(1)} %broadcast_select_fusion.3), channel_id=1, replica_groups=mesh['groups'=2,'inst'=4,'tp'=4] {'inst'}, dimensions={0}, use_global_device_ids=true | all-gather | bytes 80 | tf_op jit(solution)/shard_map/all_gather | solution.py:48
  31.8 0.6 gather_fusion.6
  32.4 0.1 reshape.239
  32.5 0.1 broadcast_select_fusion.4
  32.6 0.6 gather_fusion.7
  33.2 0.1 copy.171
  33.3 9.2 %psum.7 = f32[]{:T(128)} all-reduce(f32[]{:T(128)} %convert_reduce_fusion.1), channel_id=1, replica_groups=mesh['groups'=2,'inst'=4,'tp'=4] {'inst'}, use_global_device_ids=true, to_apply=%region_9.10 | all-reduce | flops 1 | bytes 8 | tf_op jit(solution)/shard_map/psum | solution.py:53
  42.5 0.1 fusion.24
  42.6 0.6 gather_fusion.8
  43.2 0.0 copy-start.3
  43.2 0.0 copy-start.2
  43.2 0.0 copy-start.5
  43.2 5.3 %gather_fusion.4 = bf16[32,2,2,128,128]{4,3,2,1,0:T(8,128)(2,1)} fusion(bf16[34,2,2,128,128]{4,3,2,1,0:T(8,128)(2,1)} %param.7, s32[1024]{0:T(1024)S(1)} %pad_clamp_fusion), kind=kCustom, calls=%fused_computation.4 | custom fusion | bytes 8388736 | tf_op jit(solution)/shard_map/jit(_take)/gather | solution.py:64
  48.6 0.0 copy-done.4
  48.6 0.2 copy.202
  48.8 0.1 copy.166
  48.9 0.1 convert_select_fusion
  48.9 0.1 copy.175
  49.0 0.1 copy.176
  49.1 0.0 copy-done.3
  49.1 0.1 reshape.240
  49.2 0.0 copy-done.2
  49.2 0.1 slice_reduce_fusion
  49.4 0.7 fusion.35
  50.1 0.4 copy.181
  50.6 0.1 copy.188
  50.7 0.1 copy.189
  52.1 0.1 iota_compare_fusion
  52.2 0.1 broadcast_compare_fusion
  52.3 0.0 all-gather.2.cloned.1.call-done
  52.3 1.8 %gather_fusion.2 = bf16[2,2,2,128,128]{4,3,2,1,0:T(8,128)(2,1)S(1)} fusion(bf16[8,2,2,128,128]{4,3,2,1,0:T(8,128)(2,1)} %all-gather.2.cloned.1.call-done, s32[1024]{0:T(1024)S(1)} %pad_clamp_fusion.3), kind=kCustom, calls=%fused_computation.2 | custom fusion | bytes 524296 | tf_op jit(solution)/shard_map/jit(_take)/gather | solution.py:50
  54.1 0.1 broadcast_select_fusion.2
  54.2 0.0 copy-start
  54.3 0.7 gather_fusion.3
  55.0 3.7 %fusion.2 = bf16[8,4,2,2,128,128]{5,4,1,3,0,2:T(8,128)(2,1)S(1)} fusion(bf16[8,4,2,2,128,128]{5,4,3,2,1,0:T(8,128)(2,1)} %bitcast.78, pred[8,4]{1,0:T(8,128)(4,1)S(1)} %copy.166, pred[8,4]{1,0:T(8,128)(4,1)S(1)} %fusion.24, bf16[8,2,2,128,128]{4,3,2,1,0:T(8,128)(2,1)S(1)} %gather_fusion.3, pred[8]{0:T(512)(128)(4,1)S(1)} %compare_and_fusion.1), kind=kLoop, calls=%fused_computation.12 | loop fusion | flops 4718592 | bytes 9437256 | tf_op jit(solution)/shard_map/jit(_where)/select_n | solution.py:79
  58.8 0.9 %select_reduce_fusion = (f32[8,4,2,8]{3,1,2,0:T(4,128)S(1)}, f32[8,4,2,8,4,128]{5,3,1,4,2,0:T(8,128)S(1)}) fusion(pred[8,4,128]{2,1,0:T(4,128)(4,1)S(1)} %broadcast_compare_fusion, f32[8,2,4]{2,1,0:T(2,128)S(1)} %copy.176, bf16[8,4,2,2,128,128]{5,4,1,3,0,2:T(8,128)(2,1)S(1)} %fusion.2, bf16[8,4,2,8,128]{4,3,2,1,0:T(8,128)(2,1)S(1)} %reshape.240), kind=kOutput, calls=%fused_computation.31 | convolution fusion | flops 68156928 | bytes 3291136 | tf_op jit(solution)/shard_map/sthgd,sjhkd->sthgjk/dot_general | solution.py:82
  59.7 0.2 bitcast_select_fusion
  59.8 0.4 fusion.18
  60.3 0.3 divide_convert_fusion
  60.6 0.2 copy-done.1
  60.7 0.1 slice.66
  60.8 5.8 %copy.215 = bf16[8,4,2,8,512]{3,4,1,2,0:T(8,128)(2,1)} copy(bf16[8,4,2,8,512]{4,3,2,1,0:T(8,128)(2,1)S(1)} %slice.66) | data formatting | bytes 1048576
  66.6 6.4 %fusion.11 = f32[8,2,128,4,8]{2,4,3,1,0:T(8,128)S(1)} fusion(bf16[8,4,2,8,4,128]{3,5,4,1,2,0:T(8,128)(2,1)} %bitcast.79, bf16[8,4,2,2,128,128]{5,4,1,3,0,2:T(8,128)(2,1)} %copy-done.1, f32[8,2,4]{2,1,0:T(2,128)S(1)} %copy.189), kind=kOutput, calls=%fused_computation.23 | convolution fusion | flops 67567616 | bytes 10748160 | tf_op jit(solution)/shard_map/sthgjk,sjhkd->sthgjd/dot_general | solution.py:103
  72.9 0.2 fusion.15
  73.1 0.7 reshape.323
  (24 shorter events, 0.2 us)
Async XLA Ops:
  7.2 45.1 %all-gather.2.cloned.1.call-start = ((), (), s32[]{:S(2)}) async-start(), calls=%async_computation | async-start | bytes 1310720 | tf_op jit(solution)/shard_map/all_gather | solution.py:47
  32.6 16.0 %copy-start.4 = (bf16[2,2,2]{2,1,0:T(2,128)(2,1)}, bf16[2,2,2]{2,1,0:T(2,128)(2,1)S(1)}, u32[]{:S(2)}) copy-start(bf16[2,2,2]{2,1,0:T(2,128)(2,1)S(1)} %broadcast_select_fusion.4) | copy-start | bytes 52
  43.2 5.9 %copy-start.3 = (bf16[8,4,2048]{2,1,0:T(4,128)(2,1)S(1)}, bf16[8,4,2048]{2,1,0:T(4,128)(2,1)}, u32[]{:S(2)}) copy-start(bf16[8,4,2048]{2,1,0:T(4,128)(2,1)} %param.12) | copy-start | bytes 393220
  43.2 6.0 %copy-start.2 = (bf16[8,4,2,256]{3,2,1,0:T(2,128)(2,1)S(1)}, bf16[8,4,2,256]{3,2,1,0:T(2,128)(2,1)}, u32[]{:S(2)}) copy-start(bf16[8,4,2,256]{3,2,1,0:T(2,128)(2,1)} %param.13) | copy-start | bytes 98308
  43.2 8.9 %copy-start.5 = (s32[8]{0:T(128)S(1)}, s32[8]{0:T(128)}, u32[]{:S(2)}) copy-start(s32[8]{0:T(128)} %param.9) | copy-start | bytes 100
  54.2 4.5 %copy-start = (bf16[2,2,2,128,128]{4,3,2,1,0:T(8,128)(2,1)}, bf16[2,2,2,128,128]{4,3,2,1,0:T(8,128)(2,1)S(1)}, u32[]{:S(2)}) copy-start(bf16[2,2,2,128,128]{4,3,2,1,0:T(8,128)(2,1)S(1)} %broadcast_select_fusion.2) | copy-start | bytes 786436
  58.7 2.0 %copy-start.1 = (bf16[8,4,2,2,128,128]{5,4,1,3,0,2:T(8,128)(2,1)}, bf16[8,4,2,2,128,128]{5,4,1,3,0,2:T(8,128)(2,1)S(1)}, u32[]{:S(2)}) copy-start(bf16[8,4,2,2,128,128]{5,4,1,3,0,2:T(8,128)(2,1)S(1)} %fusion.2) | copy-start | bytes 12582916
Sparse Core Ops, SparseCore 0:
  11.8 30.9 all-gather.1
where the time goes:
time: 82.2 us; the launch traced here: 81.8 us
  local copies, waits for them, and re-layouts  25.1 us (31%)
  blocking collectives  21.9 us (27%)
  between operations  16.7 us (20%)
  other arithmetic  9.83 us (12%)
  matrix products  8.1 us (10%)
    all_gather x1, blocking collectives, local(): lax.all_gather(leaving_scale, 'inst', axis=0, tiled=True)  12.7 us
    psum x1, blocking collectives, local(): total_tokens = lax.psum(tokens_here, 'inst')  9.23 us
    unnamed x18, local copies, waits for them, and re-layouts  8.25 us
    dot_general x1, matrix products, local(): jnp.einsum('sthgjk,sjhkd->sthgjd', cached_weight_rows, cached[:, :, 1], p...  6.37 us
    gather x1, local copies, waits for them, and re-layouts, local(): jnp.take(key_value_pool, flat_table, axis=0)  5.33 us
    select_n x1, other arithmetic, local(): jnp.where(last_block[:, :, None, None, None, None], arrived[:, None], cac...  3.71 us
    gather x1, local copies, waits for them, and re-layouts, local(): leaving = jnp.take(key_value_pool, own_moves[:, 0], axis=0)  2.86 us
    gather x1, local copies, waits for them, and re-layouts, local(): landed = jnp.take(every_block, arrival_row, axis=0)  1.82 us
  transfers between devices with their start and end apart: 1, of which 0 were waited for; matrix products, arithmetic and copies ran while one was open for 21% of the time, Pallas kernels for 0%

commit v1 on v0

v1 whole, which is shorter than its diff:
```python
import functools
import math

import jax
import jax.numpy as jnp
from jax import lax
from jax.experimental import pallas as pl
from jax.experimental.pallas import tpu as pltpu
from jax.sharding import PartitionSpec as P

NEG = -1e30
TRANS = (((1,), (1,)), ((), ()))


def kernel(
    n, pool_hbm, scale_hbm, lengths, table, moves, q_hbm, new_hbm,
    out_ref, landed_hbm, aux_ref,
    pool, scale, q_ref, new_ref, staged, arrived, note, notes, qs, acc_s, m_s, l_s,
    pool_sem, in_sem, send_sem, recv_sem, note_send, note_recv, land_sem,
):
    me = lax.axis_index("inst")
    slots, steps, _ = q_ref.shape
    per = staged.shape[0]
    blocks = table.shape[1]
    heads, block_len, dim = pool.shape[2:]
    group = q_ref.shape[2] // (heads * dim)
    rows = group * steps
    width = group * dim
    scaling = 1.0 / math.sqrt(dim)

    pool_copy = pltpu.make_async_copy(pool_hbm, pool, pool_sem)
    pool_copy.start()
    scale_copy = pltpu.make_async_copy(scale_hbm, scale, in_sem.at[0])
    scale_copy.start()
    q_copy = pltpu.make_async_copy(q_hbm, q_ref, in_sem.at[1])
    q_copy.start()
    new_copy = pltpu.make_async_copy(new_hbm, new_ref, in_sem.at[2])
    new_copy.start()

    barrier = pltpu.get_barrier_semaphore()
    for k in range(1, n):
        pl.semaphore_signal(
            barrier, inc=1, device_id={"inst": lax.rem(me + k, n)},
            device_id_type=pl.DeviceIdType.MESH,
        )

    tokens = jnp.float32(0.0)
    for s in range(slots):
        tokens = tokens + (lengths[s] + steps).astype(jnp.float32)
    note[per] = jnp.full((8, 128), tokens, jnp.float32)
    scale_copy.wait()
    for j in range(per):
        pair = scale[moves[me * per + j, 0]].astype(jnp.float32)
        for kv in range(2):
            for h in range(heads):
                note[j, pl.ds(kv * heads + h, 1), :] = jnp.broadcast_to(
                    pair[kv : kv + 1, h : h + 1], (1, 128)
                )
    pool_copy.wait()
    for j in range(per):
        staged[j] = pool[moves[me * per + j, 0]]
    pl.semaphore_wait(barrier, n - 1)

    sends = []
    for j in range(per):
        for kv in range(2):
            sends.append(
                pltpu.make_async_remote_copy(
                    src_ref=staged.at[j, kv], dst_ref=arrived.at[j, kv],
                    send_sem=send_sem.at[j, kv], recv_sem=recv_sem.at[j, kv],
                    device_id={"inst": lax.rem(me + 1 + j, n)},
                    device_id_type=pl.DeviceIdType.MESH,
                )
            )
    note_sends = []
    for k in range(1, n):
        note_sends.append(
            pltpu.make_async_remote_copy(
                src_ref=note, dst_ref=notes.at[k - 1],
                send_sem=note_send.at[k - 1], recv_sem=note_recv.at[k - 1],
                device_id={"inst": lax.rem(me + k, n)},
                device_id_type=pl.DeviceIdType.MESH,
            )
        )
    for copy in note_sends + sends:
        copy.start()

    sources = [lax.rem(me + n - 1 - j, n) for j in range(per)]
    arrival_rows = [sources[j] * per + j for j in range(per)]
    total_rows = n * per
    ranks = []
    for j in range(per):
        rank = 0
        for i in range(per):
            if i != j:
                rank = rank + (arrival_rows[j] - arrival_rows[i] + total_rows) // total_rows
        ranks.append(rank)
    arrival_slots = [moves[arrival_rows[j], 2] for j in range(per)]

    lane = lax.broadcasted_iota(jnp.int32, (rows, block_len), 1)
    step_of = lax.broadcasted_iota(jnp.int32, (rows, block_len), 0) % steps
    causal = lane <= step_of
    q_copy.wait()
    new_copy.wait()

    def to_lanes(o):
        return jnp.concatenate(
            [o[g * steps : (g + 1) * steps] for g in range(group)], axis=1
        ).astype(jnp.bfloat16)

    def one_slot(s, carry):
        length = lengths[s]
        count = lax.div(length + (block_len - 1), block_len)
        hit = arrival_slots[0] == s
        for j in range(1, per):
            hit = jnp.logical_or(hit, arrival_slots[j] == s)
        limit = jnp.where(hit, (count - 1) * block_len, length)
        q_all = q_ref[s].astype(jnp.float32)
        fresh = [new_ref[s, u].astype(jnp.float32) for u in range(steps)]
        index = [jnp.clip(table[s, j], 0, pool.shape[0] - 1) for j in range(blocks)]
        scales = [scale[index[j]].astype(jnp.float32) for j in range(blocks)]
        pad = jnp.zeros((block_len - steps, dim), jnp.float32)
        for h in range(heads):
            lo = h * group * dim
            qh = jnp.concatenate(
                [q_all[:, lo + g * dim : lo + (g + 1) * dim] for g in range(group)], axis=0
            ).astype(jnp.bfloat16)
            qs[s, h] = qh
            new_k, new_v = [
                jnp.concatenate(
                    [f[kv : kv + 1, h * dim : (h + 1) * dim] for f in fresh] + [pad], axis=0
                ).astype(jnp.bfloat16)
                for kv in range(2)
            ]
            scored = []
            for j in range(blocks):
                raw = lax.dot_general(
                    qh, pool[index[j], 0, h], TRANS, preferred_element_type=jnp.float32
                )
                raw = raw * (scales[j][0:1, h : h + 1] * scaling)
                scored.append(jnp.where(lane + j * block_len < limit, raw, NEG))
            raw = lax.dot_general(qh, new_k, TRANS, preferred_element_type=jnp.float32)
            scored.append(jnp.where(causal, raw * scaling, NEG))
            top = scored[0]
            for x in scored[1:]:
                top = jnp.maximum(top, x)
            top = jnp.max(top, axis=1, keepdims=True)
            p = [jnp.exp(x - top) for x in scored]
            norm = p[0]
            for x in p[1:]:
                norm = norm + x
            norm = jnp.sum(norm, axis=1, keepdims=True)
            acc = jnp.dot(p[-1].astype(jnp.bfloat16), new_v, preferred_element_type=jnp.float32)
            for j in range(blocks):
                w = (p[j] * scales[j][1:2, h : h + 1]).astype(jnp.bfloat16)
                acc = acc + jnp.dot(
                    w, pool[index[j], 1, h], preferred_element_type=jnp.float32
                )
            acc_s[s, h] = acc
            m_s[s, h] = jnp.broadcast_to(top, (rows, dim))
            l_s[s, h] = jnp.broadcast_to(norm, (rows, dim))
            out_ref[s, :, h * width : (h + 1) * width] = to_lanes(acc / norm)
        return carry

    lax.fori_loop(0, slots, one_slot, 0)

    for copy in note_sends:
        copy.wait()
    total = note[per]
    for k in range(n - 1):
        total = total + notes[k, per]
    aux_ref[per] = note[per] * n / total

    flushes = []
    for j in range(per):
        aux_ref[ranks[j]] = notes[j, j]
        slot = arrival_slots[j]
        length = lengths[slot]
        start = lax.div(length - 1, block_len) * block_len
        for kv in range(2):
            sends[2 * j + kv].wait_recv()
            flush = pltpu.make_async_copy(
                arrived.at[j, kv], landed_hbm.at[ranks[j], kv], land_sem.at[j, kv]
            )
            flush.start()
            flushes.append(flush)
        for h in range(heads):
            key_scale = notes[j, j, pl.ds(h, 1), :] * scaling
            value_scale = notes[j, j, pl.ds(heads + h, 1), :]
            raw = lax.dot_general(
                qs[slot, h], arrived[j, 0, h], TRANS, preferred_element_type=jnp.float32
            )
            x = jnp.where(lane + start < length, raw * key_scale, NEG)
            old = m_s[slot, h]
            top = jnp.maximum(old, jnp.max(x, axis=1, keepdims=True))
            fade = jnp.exp(old - top)
            p = jnp.exp(x - top)
            norm = l_s[slot, h] * fade + jnp.sum(p, axis=1, keepdims=True)
            acc = acc_s[slot, h] * fade + jnp.dot(
                (p * value_scale).astype(jnp.bfloat16), arrived[j, 1, h],
                preferred_element_type=jnp.float32,
            )
            o = to_lanes(acc / norm)
            for s in range(slots):
                part = (s, slice(None), slice(h * width, (h + 1) * width))
                out_ref[part] = jnp.where(slot == s, o, out_ref[part])
    for copy in sends:
        copy.wait_send()
    for flush in flushes:
        flush.wait()


def local(pool, scale, lengths, table, moves, queries, new_kv):
    n = lax.axis_size("inst")
    per = moves.shape[0] // n
    slots, steps, _ = queries.shape
    heads, block_len, dim = pool.shape[2:]
    rows = queries.shape[2] // (heads * dim) * steps
    any_space = pl.BlockSpec(memory_space=pl.ANY)
    smem = pl.BlockSpec(memory_space=pltpu.SMEM)
    vmem = pl.BlockSpec(memory_space=pltpu.VMEM)
    bf16, f32 = jnp.bfloat16, jnp.float32
    attended, landed, aux = pl.pallas_call(
        functools.partial(kernel, n),
        out_shape=(
            jax.ShapeDtypeStruct(queries.shape, bf16),
            jax.ShapeDtypeStruct((per,) + pool.shape[1:], bf16),
            jax.ShapeDtypeStruct((per + 1, 8, 128), f32),
        ),
        in_specs=[any_space, any_space, smem, smem, smem, any_space, any_space],
        out_specs=(vmem, any_space, vmem),
        scratch_shapes=[
            pltpu.VMEM(pool.shape, bf16),
            pltpu.VMEM(scale.shape, bf16),
            pltpu.VMEM(queries.shape, bf16),
            pltpu.VMEM(new_kv.shape, bf16),
            pltpu.VMEM((per,) + pool.shape[1:], bf16),
            pltpu.VMEM((per,) + pool.shape[1:], bf16),
            pltpu.VMEM((per + 1, 8, 128), f32),
            pltpu.VMEM((n - 1, per + 1, 8, 128), f32),
            pltpu.VMEM((slots, heads, rows, dim), bf16),
            pltpu.VMEM((slots, heads, rows, dim), f32),
            pltpu.VMEM((slots, heads, rows, dim), f32),
            pltpu.VMEM((slots, heads, rows, dim), f32),
            pltpu.SemaphoreType.DMA,
            pltpu.SemaphoreType.DMA((3,)),
            pltpu.SemaphoreType.DMA((per, 2)),
            pltpu.SemaphoreType.DMA((per, 2)),
            pltpu.SemaphoreType.DMA((n - 1,)),
            pltpu.SemaphoreType.DMA((n - 1,)),
            pltpu.SemaphoreType.DMA((per, 2)),
        ],
        compiler_params=pltpu.CompilerParams(
            collective_id=0, has_side_effects=True, vmem_limit_bytes=32 * 1024 * 1024
        ),
    )(pool, scale, lengths, table, moves, queries, new_kv)
    arrival_scales = aux[:per, : 2 * heads, 0].reshape(per, 2, heads).astype(bf16)
    load = aux[per, 0, :1]
    return attended, landed, arrival_scales, load


def solution(mesh):
    both = ("groups", "inst")
    return jax.shard_map(
        local,
        mesh=mesh,
        in_specs=(
            P(both, None, "tp", None, None),
            P(both, None, "tp"),
            P(both),
            P(both, None),
            P("groups", None),
            P(both, None, "tp"),
            P(both, None, None, "tp"),
        ),
        out_specs=(
            P(both, None, "tp"),
            P(both, None, "tp", None, None),
            P(both, None, "tp"),
            P(both),
        ),
        check_vma=False,
    )
```

time: 82.2 us -> 27.9 us (0.34)
  blocking collectives: 21.9 us -> 0 us
  Pallas kernels: 0 us -> 17.5 us
  between operations: 16.7 us -> 0.65 us
  local copies, waits for them, and re-layouts: 25.1 us -> 9.5 us
  other arithmetic: 9.83 us -> 0 us
  matrix products: 8.1 us -> 0 us
    pallas_call x0 -> x1, Pallas kernels: none -> 17.5 us  [local(): pl.pallas_call(functools.partial(kernel, n), out_shape=(jax.ShapeDtypeStr...]
    gather x11 -> x0, local copies, waits for them, and re-layouts: 14 us -> none  [the longest x1 5.33 us: local(): jnp.take(key_value_pool, flat_table, axis=0)]
    all_gather x1 -> x0, blocking collectives: 12.7 us -> none  [local(): lax.all_gather(leaving_scale, 'inst', axis=0, tiled=True)]
    psum x1 -> x0, blocking collectives: 9.23 us -> none  [local(): total_tokens = lax.psum(tokens_here, 'inst')]
    dot_general x4 -> x0, matrix products: 8.1 us -> none  [the longest x1 6.37 us: local(): jnp.einsum('sthgjk,sjhkd->sthgjd', cached_weight_rows, cached[:, :, 1], p...]
    select_n x12 -> x0, other arithmetic: 5.02 us -> none  [the longest x1 3.71 us: local(): jnp.where(last_block[:, :, None, None, None, None], arrived[:, None], cac...]
    reduce_sum x5 -> x0, other arithmetic: 2.08 us -> none  [the longest x1 1.26 us: local(): tokens_here = jnp.sum((lengths + steps).astype(jnp.float32))]
    and x4 -> x0, other arithmetic: 1.46 us -> none  [the longest x1 0.69 us: local(): (targets == my_index)[:, None] & (rank[:, None] == ranks_here[None, :])]
  transfers between devices with their start and end apart: 1 -> 0, of which waited for: 0 -> 0; matrix products, arithmetic and copies ran while one was open for 21% -> 0% of each run, Pallas kernels for 0% -> 0%
where the time goes in v1:
time: 27.9 us; the launch traced here: 27.6 us
  Pallas kernels  17.5 us (63%)
  local copies, waits for them, and re-layouts  9.5 us (34%)
  between operations  0.65 us (2%)
    pallas_call x1, Pallas kernels, local(): pl.pallas_call(functools.partial(kernel, n), out_shape=(jax.ShapeDtypeStr...  17.5 us
    unnamed x13, local copies, waits for them, and re-layouts  8.25 us
    convert_element_type x1, local copies, waits for them, and re-layouts, local(): aux[:per, :2 * heads, 0].reshape(per, 2, heads).astype(bf16)  0.65 us

profile of v1, /device:TPU:0, one launch (start us, length us, event | category | flops | bytes accessed | tf_op | source)
XLA Modules:
  0.0 27.6 jit_solution(17123873859998407419)
XLA Ops:
  0.6 0.8 %copy.15.table = s32[8,4]{1,0:T(8,128)S(1)} copy(s32[8,4]{0,1:T(4,128)} %param.10) | data formatting | bytes 256 | tf_op args[3]
  1.4 0.8 %copy.16.moves = s32[8,3]{1,0:T(8,128)S(1)} copy(s32[8,3]{0,1:T(4,128)} %param.11) | data formatting | bytes 192 | tf_op args[4]
  2.1 0.8 %copy.14.scale_hbm = bf16[34,2,2]{2,1,0:T(2,128)(2,1)S(1)} copy(bf16[34,2,2]{0,2,1:T(2,128)(2,1)} %param.8) | data formatting | bytes 544 | tf_op args[1]
  2.9 0.0 copy-start
  2.9 2.3 %copy-done = bf16[34,2,2,128,128]{4,3,2,1,0:T(8,128)(2,1)S(1)} copy-done((bf16[34,2,2,128,128]{4,3,2,1,0:T(8,128)(2,1)S(1)}, bf16[34,2,2,128,128]{4,3,2,1,0:T(8,128)(2,1)}, u32[]{:S(2)}) %copy-start) | copy-done | bytes 4456472
  5.2 0.0 copy-start.1
  5.2 0.9 %copy-done.1 = bf16[8,4,2048]{2,1,0:T(4,128)(2,1)S(1)} copy-done((bf16[8,4,2048]{2,1,0:T(4,128)(2,1)S(1)}, bf16[8,4,2048]{2,1,0:T(4,128)(2,1)}, u32[]{:S(2)}) %copy-start.1) | copy-done | bytes 131096
  6.1 0.0 copy-start.2
  6.1 0.8 %copy-done.2 = bf16[8,4,2,256]{3,2,1,0:T(2,128)(2,1)S(1)} copy-done((bf16[8,4,2,256]{3,2,1,0:T(2,128)(2,1)S(1)}, bf16[8,4,2,256]{3,2,1,0:T(2,128)(2,1)}, u32[]{:S(2)}) %copy-start.2) | copy-done | bytes 32792
  6.9 0.0 copy-start.3
  6.9 0.7 %copy-done.3 = s32[8]{0:T(128)S(1)} copy-done((s32[8]{0:T(128)S(1)}, s32[8]{0:T(128)}, u32[]{:S(2)}) %copy-start.3) | copy-done | bytes 56
  7.5 17.5 %shard_map.102 = (bf16[8,4,2048]{2,1,0:T(4,128)(2,1)S(1)}, bf16[2,2,2,128,128]{4,3,2,1,0:T(8,128)(2,1)S(1)}, f32[3,8,128]{2,1,0:T(8,128)S(1)}) custom-call(bf16[34,2,2,128,128]{4,3,2,1,0:T(8,128)(2,1)S(1)} %copy-done, bf16[34,2,2]{2,1,0:T(2,128)(2,1)S(1)} %copy.14.scale_hbm, s32[8]{0:T(128)S(1)} %copy-done.3, s32[8,4]{1,0:T(8,128)S(1)} %copy.15.table, ...), custom_call_target="tpu_custom_call" | custom-call | tf_op jit(solution)/shard_map/pallas_call | solution.py:223
  25.0 0.5 %slice.8 = f32[1,1,1]{2,1,0:T(1,128)} slice(f32[3,8,128]{2,1,0:T(8,128)S(1)} %get-tuple-element.9), slice={[2:3], [0:1], [0:1]} | slice | bytes 8 | tf_op jit(solution)/shard_map/slice | solution.py:258
  25.5 0.1 fusion
  25.6 0.6 %convert_element_type.4 = bf16[2,2,2]{2,1,0:T(2,128)(2,1)} reshape(bf16[2,4]{1,0:T(2,128)(2,1)S(1)} %fusion) | data formatting | bytes 32 | tf_op jit(solution)/shard_map/convert_element_type | solution.py:257
  26.3 0.7 %copy.19 = bf16[8,4,2048]{2,1,0:T(4,128)(2,1)} copy(bf16[8,4,2048]{2,1,0:T(4,128)(2,1)S(1)} %get-tuple-element.14) | data formatting | bytes 262144
  26.9 0.7 %copy.20 = bf16[2,2,2,128,128]{4,3,2,1,0:T(8,128)(2,1)} copy(bf16[2,2,2,128,128]{4,3,2,1,0:T(8,128)(2,1)S(1)} %get-tuple-element.15) | data formatting | bytes 524288
Async XLA Ops:
  2.9 2.3 %copy-start = (bf16[34,2,2,128,128]{4,3,2,1,0:T(8,128)(2,1)S(1)}, bf16[34,2,2,128,128]{4,3,2,1,0:T(8,128)(2,1)}, u32[]{:S(2)}) copy-start(bf16[34,2,2,128,128]{4,3,2,1,0:T(8,128)(2,1)} %pool_hbm.1) | copy-start | bytes 13369348
  5.2 0.9 %copy-start.1 = (bf16[8,4,2048]{2,1,0:T(4,128)(2,1)S(1)}, bf16[8,4,2048]{2,1,0:T(4,128)(2,1)}, u32[]{:S(2)}) copy-start(bf16[8,4,2048]{2,1,0:T(4,128)(2,1)} %q_hbm.1) | copy-start | bytes 393220
  6.1 0.8 %copy-start.2 = (bf16[8,4,2,256]{3,2,1,0:T(2,128)(2,1)S(1)}, bf16[8,4,2,256]{3,2,1,0:T(2,128)(2,1)}, u32[]{:S(2)}) copy-start(bf16[8,4,2,256]{3,2,1,0:T(2,128)(2,1)} %new_hbm.1) | copy-start | bytes 98308
  6.9 0.7 %copy-start.3 = (s32[8]{0:T(128)S(1)}, s32[8]{0:T(128)}, u32[]{:S(2)}) copy-start(s32[8]{0:T(128)} %lengths.1) | copy-start | bytes 100

commit v2 on v1

v2 whole, which is shorter than its diff:
```python
import functools
import math

import jax
import jax.numpy as jnp
from jax import lax
from jax.experimental import pallas as pl
from jax.experimental.pallas import tpu as pltpu
from jax.sharding import PartitionSpec as P

NEG = -1e30
TRANS = (((1,), (1,)), ((), ()))


def to_lanes(o, steps):
    return jnp.concatenate(
        [o[i : i + steps] for i in range(0, o.shape[0], steps)], axis=1
    ).astype(jnp.bfloat16)


def kernel(
    n, pool_hbm, scale_hbm, lengths_hbm, table_hbm, moves_hbm, q_hbm, new_hbm,
    out_ref, arrived, q_out, acc_out, m_out, l_out, info_ref, load_ref,
    pool, scale, lengths, table, moves, q_ref, new_ref, staged, note, notes, qs, acc_s, m_s, l_s,
    pool_sem, in_sem, send_sem, recv_sem, note_send, note_recv,
):
    me = lax.axis_index("inst")
    slots, steps, _ = q_ref.shape
    per = staged.shape[0]
    blocks = table.shape[0]
    heads, block_len, dim = pool.shape[2:]
    group = q_ref.shape[2] // (heads * dim)
    rows = group * steps
    width = group * dim
    scaling = 1.0 / math.sqrt(dim)

    barrier = pltpu.get_barrier_semaphore()
    for k in range(1, n):
        pl.semaphore_signal(
            barrier, inc=1, device_id={"inst": lax.rem(me + k, n)},
            device_id_type=pl.DeviceIdType.MESH,
        )
    small = [
        pltpu.make_async_copy(x, y, in_sem.at[3 + i])
        for i, (x, y) in enumerate(
            ((moves_hbm, moves), (lengths_hbm, lengths), (table_hbm, table))
        )
    ]
    for copy in small:
        copy.start()
    pool_copy = pltpu.make_async_copy(pool_hbm, pool, pool_sem)
    pool_copy.start()
    scale_copy = pltpu.make_async_copy(scale_hbm, scale, in_sem.at[0])
    scale_copy.start()
    q_copy = pltpu.make_async_copy(q_hbm, q_ref, in_sem.at[1])
    q_copy.start()
    new_copy = pltpu.make_async_copy(new_hbm, new_ref, in_sem.at[2])
    new_copy.start()

    for copy in small:
        copy.wait()

    tokens = jnp.float32(0.0)
    for s in range(slots):
        tokens = tokens + (lengths[s] + steps).astype(jnp.float32)
    note[per] = jnp.full((8, 128), tokens, jnp.float32)
    scale_copy.wait()
    scale_rows = jnp.concatenate(
        [scale[kv].astype(jnp.float32) for kv in range(2)], axis=0
    )
    block_of = lax.broadcasted_iota(jnp.int32, scale_rows.shape, 1)

    def block_scale(index):
        return jnp.sum(
            jnp.where(block_of == index, scale_rows, 0.0), axis=1, keepdims=True
        )

    head_lane = lax.broadcasted_iota(jnp.int32, (1, 128), 1)
    for j in range(per):
        pair = block_scale(moves[0, me * per + j])
        for kv in range(2):
            row = jnp.zeros((1, 128), jnp.float32)
            for h in range(heads):
                r = kv * heads + h
                row = jnp.where(head_lane == h, pair[r : r + 1], row)
            note[j, pl.ds(kv, 1), :] = row
    pool_copy.wait()
    for j in range(per):
        staged[j] = pool[moves[0, me * per + j]]
    pl.semaphore_wait(barrier, n - 1)

    sends = []
    for j in range(per):
        for kv in range(2):
            sends.append(
                pltpu.make_async_remote_copy(
                    src_ref=staged.at[j, kv], dst_ref=arrived.at[j, kv],
                    send_sem=send_sem.at[j, kv], recv_sem=recv_sem.at[j, kv],
                    device_id={"inst": lax.rem(me + 1 + j, n)},
                    device_id_type=pl.DeviceIdType.MESH,
                )
            )
    note_sends = []
    for k in range(1, n):
        note_sends.append(
            pltpu.make_async_remote_copy(
                src_ref=note, dst_ref=notes.at[k - 1],
                send_sem=note_send.at[k - 1], recv_sem=note_recv.at[k - 1],
                device_id={"inst": lax.rem(me + k, n)},
                device_id_type=pl.DeviceIdType.MESH,
            )
        )
    for copy in note_sends + sends:
        copy.start()

    sources = [lax.rem(me + n - 1 - j, n) for j in range(per)]
    arrival_rows = [sources[j] * per + j for j in range(per)]
    arrival_slots = [moves[2, arrival_rows[j]] for j in range(per)]

    lane = lax.broadcasted_iota(jnp.int32, (rows, block_len), 1)
    step_of = lax.broadcasted_iota(jnp.int32, (rows, block_len), 0) % steps
    causal = lane <= step_of
    q_copy.wait()
    new_copy.wait()

    def one_slot(s, carry):
        length = lengths[s]
        count = lax.div(length + (block_len - 1), block_len)
        hit = arrival_slots[0] == s
        for j in range(1, per):
            hit = jnp.logical_or(hit, arrival_slots[j] == s)
        limit = jnp.where(hit, (count - 1) * block_len, length)
        q_all = q_ref[s].astype(jnp.float32)
        fresh = [new_ref[s, u].astype(jnp.float32) for u in range(steps)]
        index = [jnp.clip(table[j, s], 0, pool.shape[0] - 1) for j in range(blocks)]
        scales = [block_scale(index[j]) for j in range(blocks)]
        pad = jnp.zeros((block_len - steps, dim), jnp.float32)
        for h in range(heads):
            lo = h * group * dim
            qh = jnp.concatenate(
                [q_all[:, lo + g * dim : lo + (g + 1) * dim] for g in range(group)], axis=0
            ).astype(jnp.bfloat16)
            qs[s, h] = qh
            new_k, new_v = [
                jnp.concatenate(
                    [f[kv : kv + 1, h * dim : (h + 1) * dim] for f in fresh] + [pad], axis=0
                ).astype(jnp.bfloat16)
                for kv in range(2)
            ]
            scored = []
            for j in range(blocks):
                raw = lax.dot_general(
                    qh, pool[index[j], 0, h], TRANS, preferred_element_type=jnp.float32
                )
                raw = raw * (scales[j][h : h + 1] * scaling)
                scored.append(jnp.where(lane + j * block_len < limit, raw, NEG))
            raw = lax.dot_general(qh, new_k, TRANS, preferred_element_type=jnp.float32)
            scored.append(jnp.where(causal, raw * scaling, NEG))
            top = scored[0]
            for x in scored[1:]:
                top = jnp.maximum(top, x)
            top = jnp.max(top, axis=1, keepdims=True)
            p = [jnp.exp(x - top) for x in scored]
            norm = p[0]
            for x in p[1:]:
                norm = norm + x
            norm = jnp.sum(norm, axis=1, keepdims=True)
            acc = jnp.dot(p[-1].astype(jnp.bfloat16), new_v, preferred_element_type=jnp.float32)
            for j in range(blocks):
                w = (p[j] * scales[j][heads + h : heads + h + 1]).astype(jnp.bfloat16)
                acc = acc + jnp.dot(
                    w, pool[index[j], 1, h], preferred_element_type=jnp.float32
                )
            acc_s[s, h] = acc
            m_s[s, h] = jnp.broadcast_to(top, (rows, dim))
            l_s[s, h] = jnp.broadcast_to(norm, (rows, dim))
            out_ref[s, :, h * width : (h + 1) * width] = to_lanes(acc / norm, steps)
        return carry

    lax.fori_loop(0, slots, one_slot, 0)

    for copy in note_sends:
        copy.wait()
    total = note[per]
    for k in range(n - 1):
        total = total + notes[k, per]
    load_ref[...] = note[per] * n / total
    row_of = lax.broadcasted_iota(jnp.int32, (8, 128), 0)
    for j in range(per):
        slot = arrival_slots[j]
        length = lengths[slot]
        start = lax.div(length - 1, block_len) * block_len
        q_out[j] = qs[slot]
        acc_out[j] = acc_s[slot]
        m_out[j] = m_s[slot]
        l_out[j] = l_s[slot]
        info = jnp.where(lane[:8] + start < length, 0.0, NEG)
        info = jnp.where(row_of == 1, slot.astype(jnp.float32), info)
        for kv in range(2):
            for h in range(heads):
                info = jnp.where(
                    row_of == 2 + kv * heads + h, notes[j, j][kv : kv + 1, h : h + 1], info
                )
        info_ref[j] = info
    for copy in sends:
        copy.wait()


def merge_kernel(
    n, att, arrived, q, acc_in, m_in, l_in, info, load_tile,
    out_ref, landed_hbm, arrival_ref, load_ref, land_sem,
):
    me = lax.axis_index("inst")
    slots, steps, _ = att.shape
    per, heads, rows, dim = q.shape
    width = rows // steps * dim
    scaling = 1.0 / math.sqrt(dim)
    arrival_rows = [lax.rem(me + n - 1 - j, n) * per + j for j in range(per)]
    total_rows = n * per
    ranks = []
    for j in range(per):
        rank = 0
        for i in range(per):
            if i != j:
                rank = rank + (arrival_rows[j] - arrival_rows[i] + total_rows) // total_rows
        ranks.append(rank)
    copies = [
        pltpu.make_async_copy(arrived.at[j], landed_hbm.at[ranks[j]], land_sem.at[j])
        for j in range(per)
    ]
    for copy in copies:
        copy.start()
    load_ref[0] = load_tile[...][0, 0]
    lane = lax.broadcasted_iota(jnp.int32, (2, heads), 1)
    kv_of = lax.broadcasted_iota(jnp.int32, (2, heads), 0)
    for j in range(per):
        tile = jnp.zeros((2, heads), jnp.float32)
        for kv in range(2):
            for h in range(heads):
                r = 2 + kv * heads + h
                tile = jnp.where((kv_of == kv) & (lane == h), info[j, r : r + 1, 0:1], tile)
        arrival_ref[ranks[j]] = tile.astype(jnp.bfloat16)
    for h in range(heads):
        merged = []
        for j in range(per):
            raw = lax.dot_general(
                q[j, h], arrived[j, 0, h], TRANS, preferred_element_type=jnp.float32
            )
            x = raw * (info[j, 2 + h : 3 + h, :] * scaling)
            x = jnp.where(info[j, 0:1, :] < 0.0, NEG, x)
            old = m_in[j, h]
            top = jnp.maximum(old, jnp.max(x, axis=1, keepdims=True))
            fade = jnp.exp(old - top)
            p = jnp.exp(x - top)
            norm = l_in[j, h] * fade + jnp.sum(p, axis=1, keepdims=True)
            r = 2 + heads + h
            acc = acc_in[j, h] * fade + jnp.dot(
                (p * info[j, r : r + 1, :]).astype(jnp.bfloat16), arrived[j, 1, h],
                preferred_element_type=jnp.float32,
            )
            merged.append(to_lanes(acc / norm, steps))
        for s in range(slots):
            part = (s, slice(None), slice(h * width, (h + 1) * width))
            value = att[part]
            for j in range(per):
                hit = jnp.broadcast_to(info[j, 1:2, 0:1], merged[j].shape) == float(s)
                value = jnp.where(hit, merged[j], value)
            out_ref[part] = value
    for copy in copies:
        copy.wait()


def local(pool, scale, lengths, table, moves, queries, new_kv):
    n = lax.axis_size("inst")
    per = moves.shape[0] // n
    slots, steps, _ = queries.shape
    heads, block_len, dim = pool.shape[2:]
    rows = queries.shape[2] // (heads * dim) * steps
    hbm = functools.partial(pltpu.with_memory_space_constraint, memory_space=pltpu.HBM)
    any_space = pl.BlockSpec(memory_space=pl.ANY)
    smem = pl.BlockSpec(memory_space=pltpu.SMEM)
    vmem = pl.BlockSpec(memory_space=pltpu.VMEM)
    bf16, f32 = jnp.bfloat16, jnp.float32
    outs = (
        jax.ShapeDtypeStruct(queries.shape, bf16),
        jax.ShapeDtypeStruct((per,) + pool.shape[1:], bf16),
        jax.ShapeDtypeStruct((per, 2, heads), bf16),
        jax.ShapeDtypeStruct((1,), f32),
    )
    state = jax.ShapeDtypeStruct((per, heads, rows, dim), f32)
    results = pl.pallas_call(
        functools.partial(kernel, n),
        out_shape=(
            jax.ShapeDtypeStruct(queries.shape, bf16),
            jax.ShapeDtypeStruct((per,) + pool.shape[1:], bf16),
            jax.ShapeDtypeStruct((per, heads, rows, dim), bf16),
            state, state, state,
            jax.ShapeDtypeStruct((per, 8, 128), f32),
            jax.ShapeDtypeStruct((8, 128), f32),
        ),
        in_specs=[any_space] * 7,
        out_specs=(vmem,) * 8,
        scratch_shapes=[
            pltpu.VMEM(pool.shape, bf16),
            pltpu.VMEM(scale.shape[1:] + scale.shape[:1], bf16),
            pltpu.SMEM(lengths.shape, jnp.int32),
            pltpu.SMEM(table.shape[::-1], jnp.int32),
            pltpu.SMEM(moves.shape[::-1], jnp.int32),
            pltpu.VMEM(queries.shape, bf16),
            pltpu.VMEM(new_kv.shape, bf16),
            pltpu.VMEM((per,) + pool.shape[1:], bf16),
            pltpu.VMEM((per + 1, 8, 128), f32),
            pltpu.VMEM((n - 1, per + 1, 8, 128), f32),
            pltpu.VMEM((slots, heads, rows, dim), bf16),
            pltpu.VMEM((slots, heads, rows, dim), f32),
            pltpu.VMEM((slots, heads, rows, dim), f32),
            pltpu.VMEM((slots, heads, rows, dim), f32),
            pltpu.SemaphoreType.DMA,
            pltpu.SemaphoreType.DMA((6,)),
            pltpu.SemaphoreType.DMA((per, 2)),
            pltpu.SemaphoreType.DMA((per, 2)),
            pltpu.SemaphoreType.DMA((n - 1,)),
            pltpu.SemaphoreType.DMA((n - 1,)),
        ],
        compiler_params=pltpu.CompilerParams(
            collective_id=0, has_side_effects=True, vmem_limit_bytes=32 * 1024 * 1024
        ),
    )(
        hbm(pool), hbm(jnp.transpose(scale, (1, 2, 0))), hbm(lengths), hbm(table.T), hbm(moves.T),
        hbm(queries), hbm(new_kv),
    )
    return pl.pallas_call(
        functools.partial(merge_kernel, n),
        out_shape=outs,
        in_specs=[vmem] * 8,
        out_specs=(vmem, any_space, vmem, smem),
        scratch_shapes=[pltpu.SemaphoreType.DMA((per,))],
        compiler_params=pltpu.CompilerParams(vmem_limit_bytes=32 * 1024 * 1024),
    )(*results)


def solution(mesh):
    both = ("groups", "inst")
    return jax.shard_map(
        local,
        mesh=mesh,
        in_specs=(
            P(both, None, "tp", None, None),
            P(both, None, "tp"),
            P(both),
            P(both, None),
            P("groups", None),
            P(both, None, "tp"),
            P(both, None, None, "tp"),
        ),
        out_specs=(
            P(both, None, "tp"),
            P(both, None, "tp", None, None),
            P(both, None, "tp"),
            P(both),
        ),
        check_vma=False,
    )
```

time: 27.9 us -> 20 us (0.72)
  local copies, waits for them, and re-layouts: 9.5 us -> 0 us
  Pallas kernels: 17.5 us -> 19.2 us
    unnamed x13 -> x0, local copies, waits for them, and re-layouts: 8.25 us -> none
    pallas_call x0 -> x1, Pallas kernels: none -> 2.39 us  [local(): pl.pallas_call(functools.partial(merge_kernel, n), out_shape=outs, in_spe...]
    convert_element_type x1 -> x0, local copies, waits for them, and re-layouts: 0.65 us -> none  [local(): aux[:per, :2 * heads, 0].reshape(per, 2, heads).astype(bf16)]
    pallas_call x1, Pallas kernels: 17.5 us -> 16.8 us  [local(): pl.pallas_call(functools.partial(kernel, n), out_shape=(jax.ShapeDtypeStr...]
    slice x2 -> x0, local copies, waits for them, and re-layouts: 0.6 us -> none  [the longest x1 0.51 us: local(): load = aux[per, 0, :1]]
where the time goes in v2:
time: 20 us; the launch traced here: 19.9 us
  Pallas kernels  19.2 us (96%)
  between operations  0.64 us (3%)
    pallas_call x1, Pallas kernels, local(): pl.pallas_call(functools.partial(kernel, n), out_shape=(jax.ShapeDtypeStr...  16.8 us
    pallas_call x1, Pallas kernels, local(): pl.pallas_call(functools.partial(merge_kernel, n), out_shape=outs, in_spe...  2.39 us

profile of v2, /device:TPU:0, one launch (start us, length us, event | category | flops | bytes accessed | tf_op | source)
XLA Modules:
  0.0 19.9 jit_solution(14683115104724176961)
XLA Ops:
  0.6 16.8 %shard_map.102 = (bf16[8,4,2048]{2,1,0:T(4,128)(2,1)S(1)}, bf16[2,2,2,128,128]{4,3,2,1,0:T(8,128)(2,1)S(1)}, bf16[2,2,32,128]{3,2,1,0:T(8,128)(2,1)S(1)}, f32[2,...) custom-call(bf16[34,2,2,128,128]{4,3,2,1,0:T(8,128)(2,1)} %pool_hbm., ...), custom_call_target="tpu_custom_call" | custom-call | tf_op jit(solution)/shard_map/pallas_call | solution.py:291
  17.5 2.4 %shard_map.103 = (bf16[8,4,2048]{2,1,0:T(4,128)(2,1)}, bf16[2,2,2,128,128]{4,3,2,1,0:T(8,128)(2,1)}, bf16[2,2,2]{2,1,0:T(2,128)(2,1)}, f32[1]{0:T(128)}) custom-call(bf16[8,4,2048]{2,1,0:T(4,128)(2,1)S(1)} %get-tuple-element.12.att, bf16[2,2,2,128,128]{4,3,2,1,0:T(8,128)(2,1)S(1)} %get-tuple-element.13.arrived, ...), custom_call_target="tpu_custom_call" | custom-call | tf_op jit(solution)/shard_map/pallas_call | solution.py:332

commit v3 on v2

--- a/solution.py
+++ b/solution.py
@@ -20,7 +20,7 @@
 
 def kernel(
     n, pool_hbm, scale_hbm, lengths_hbm, table_hbm, moves_hbm, q_hbm, new_hbm,
-    out_ref, arrived, q_out, acc_out, m_out, l_out, info_ref, load_ref,
+    out_ref, arrived, p_out, acc_out, info_ref, arrival_ref, load_ref,
     pool, scale, lengths, table, moves, q_ref, new_ref, staged, note, notes, qs, acc_s, m_s, l_s,
     pool_sem, in_sem, send_sem, recv_sem, note_send, note_recv,
 ):
@@ -34,6 +34,16 @@
     width = group * dim
     scaling = 1.0 / math.sqrt(dim)
 
+    pieces = pool_sem.shape[0]
+    edges = [pool.shape[0] * i // pieces for i in range(pieces + 1)]
+    pool_copies = []
+    for i in range(pieces):
+        part = pl.ds(edges[i], edges[i + 1] - edges[i])
+        pool_copies.append(
+            pltpu.make_async_copy(pool_hbm.at[part], pool.at[part], pool_sem.at[i])
+        )
+    for copy in pool_copies:
+        copy.start()
     barrier = pltpu.get_barrier_semaphore()
     for k in range(1, n):
         pl.semaphore_signal(
@@ -48,8 +58,6 @@
     ]
     for copy in small:
         copy.start()
-    pool_copy = pltpu.make_async_copy(pool_hbm, pool, pool_sem)
-    pool_copy.start()
     scale_copy = pltpu.make_async_copy(scale_hbm, scale, in_sem.at[0])
     scale_copy.start()
     q_copy = pltpu.make_async_copy(q_hbm, q_ref, in_sem.at[1])
@@ -84,7 +92,8 @@
                 r = kv * heads + h
                 row = jnp.where(head_lane == h, pair[r : r + 1], row)
             note[j, pl.ds(kv, 1), :] = row
-    pool_copy.wait()
+    for copy in pool_copies:
+        copy.wait()
     for j in range(per):
         staged[j] = pool[moves[0, me * per + j]]
     pl.semaphore_wait(barrier, n - 1)
@@ -110,8 +119,14 @@
                 device_id_type=pl.DeviceIdType.MESH,
             )
         )
-    for copy in note_sends + sends:
-        copy.start()
+    for copy in note_sends + sends[:2]:
+        copy.start()
+    last = me == n - 1
+
+    @pl.when(jnp.logical_not(last))
+    def _():
+        for copy in sends[2:]:
+            copy.start()
 
     sources = [lax.rem(me + n - 1 - j, n) for j in range(per)]
     arrival_rows = [sources[j] * per + j for j in range(per)]
@@ -177,7 +192,16 @@
             out_ref[s, :, h * width : (h + 1) * width] = to_lanes(acc / norm, steps)
         return carry
 
-    lax.fori_loop(0, slots, one_slot, 0)
+    held = slots * 7 // 8
+    lax.fori_loop(0, held, one_slot, 0)
+
+    @pl.when(last)
+    def _():
+        for copy in sends[2:]:
+            copy.start()
+
+    if held < slots:
+        lax.fori_loop(held, slots, one_slot, 0)
 
     for copy in note_sends:
         copy.wait()
@@ -185,36 +209,48 @@
     for k in range(n - 1):
         total = total + notes[k, per]
     load_ref[...] = note[per] * n / total
-    row_of = lax.broadcasted_iota(jnp.int32, (8, 128), 0)
+    total_rows = n * per
+    ranks = []
+    for j in range(per):
+        rank = 0
+        for i in range(per):
+            if i != j:
+                rank = rank + (arrival_rows[j] - arrival_rows[i] + total_rows) // total_rows
+        ranks.append(rank)
     for j in range(per):
         slot = arrival_slots[j]
         length = lengths[slot]
         start = lax.div(length - 1, block_len) * block_len
-        q_out[j] = qs[slot]
-        acc_out[j] = acc_s[slot]
-        m_out[j] = m_s[slot]
-        l_out[j] = l_s[slot]
-        info = jnp.where(lane[:8] + start < length, 0.0, NEG)
-        info = jnp.where(row_of == 1, slot.astype(jnp.float32), info)
-        for kv in range(2):
-            for h in range(heads):
-                info = jnp.where(
-                    row_of == 2 + kv * heads + h, notes[j, j][kv : kv + 1, h : h + 1], info
-                )
-        info_ref[j] = info
+        info_ref[j] = jnp.full((8, 128), slot.astype(jnp.float32), jnp.float32)
+        tile = notes[j, j]
+        arrival_ref[ranks[j]] = tile[:2, :heads].astype(jnp.bfloat16)
+        sends[2 * j].wait_recv()
+        for h in range(heads):
+            raw = lax.dot_general(
+                qs[slot, h], arrived[j, 0, h], TRANS, preferred_element_type=jnp.float32
+            )
+            x = jnp.where(lane + start < length, raw * (tile[0:1, h : h + 1] * scaling), NEG)
+            old = m_s[slot, h]
+            top = jnp.maximum(old, jnp.max(x, axis=1, keepdims=True))
+            fade = jnp.exp(old - top)
+            p = jnp.exp(x - top)
+            norm = l_s[slot, h] * fade + jnp.sum(p, axis=1, keepdims=True)
+            p_out[j, h] = (p * (tile[1:2, h : h + 1] / norm)).astype(jnp.bfloat16)
+            acc_out[j, h] = acc_s[slot, h] * (fade / norm)
+    for j in range(per):
+        sends[2 * j + 1].wait_recv()
     for copy in sends:
-        copy.wait()
+        copy.wait_send()
 
 
 def merge_kernel(
-    n, att, arrived, q, acc_in, m_in, l_in, info, load_tile,
-    out_ref, landed_hbm, arrival_ref, load_ref, land_sem,
+    n, att, arrived, p_in, acc_in, info, arrival, load_tile,
+    out_hbm, landed_hbm, arrival_hbm, load_hbm, out_ref, load_ref, land_sem, small_sem, out_sem,
 ):
     me = lax.axis_index("inst")
     slots, steps, _ = att.shape
-    per, heads, rows, dim = q.shape
+    per, heads, rows, dim = p_in.shape
     width = rows // steps * dim
-    scaling = 1.0 / math.sqrt(dim)
     arrival_rows = [lax.rem(me + n - 1 - j, n) * per + j for j in range(per)]
     total_rows = n * per
     ranks = []
@@ -228,37 +264,22 @@
         pltpu.make_async_copy(arrived.at[j], landed_hbm.at[ranks[j]], land_sem.at[j])
         for j in range(per)
     ]
+    copies.append(pltpu.make_async_copy(arrival, arrival_hbm, small_sem.at[0]))
     for copy in copies:
         copy.start()
     load_ref[0] = load_tile[...][0, 0]
-    lane = lax.broadcasted_iota(jnp.int32, (2, heads), 1)
-    kv_of = lax.broadcasted_iota(jnp.int32, (2, heads), 0)
-    for j in range(per):
-        tile = jnp.zeros((2, heads), jnp.float32)
-        for kv in range(2):
-            for h in range(heads):
-                r = 2 + kv * heads + h
-                tile = jnp.where((kv_of == kv) & (lane == h), info[j, r : r + 1, 0:1], tile)
-        arrival_ref[ranks[j]] = tile.astype(jnp.bfloat16)
+    load_copy = pltpu.make_async_copy(load_ref, load_hbm, small_sem.at[1])
+    load_copy.start()
+    copies.append(load_copy)
     for h in range(heads):
-        merged = []
-        for j in range(per):
-            raw = lax.dot_general(
-                q[j, h], arrived[j, 0, h], TRANS, preferred_element_type=jnp.float32
+        merged = [
+            to_lanes(
+                acc_in[j, h]
+                + jnp.dot(p_in[j, h], arrived[j, 1, h], preferred_element_type=jnp.float32),
+                steps,
             )
-            x = raw * (info[j, 2 + h : 3 + h, :] * scaling)
-            x = jnp.where(info[j, 0:1, :] < 0.0, NEG, x)
-            old = m_in[j, h]
-            top = jnp.maximum(old, jnp.max(x, axis=1, keepdims=True))
-            fade = jnp.exp(old - top)
-            p = jnp.exp(x - top)
-            norm = l_in[j, h] * fade + jnp.sum(p, axis=1, keepdims=True)
-            r = 2 + heads + h
-            acc = acc_in[j, h] * fade + jnp.dot(
-                (p * info[j, r : r + 1, :]).astype(jnp.bfloat16), arrived[j, 1, h],
-                preferred_element_type=jnp.float32,
-            )
-            merged.append(to_lanes(acc / norm, steps))
+            for j in range(per)
+        ]
         for s in range(slots):
             part = (s, slice(None), slice(h * width, (h + 1) * width))
             value = att[part]
@@ -266,6 +287,10 @@
                 hit = jnp.broadcast_to(info[j, 1:2, 0:1], merged[j].shape) == float(s)
                 value = jnp.where(hit, merged[j], value)
             out_ref[part] = value
+        half = (slice(None), slice(None), pl.ds(h * width, width))
+        copy = pltpu.make_async_copy(out_ref.at[half], out_hbm.at[half], out_sem.at[h])
+        copy.start()
+        copies.append(copy)
     for copy in copies:
         copy.wait()
 
@@ -278,7 +303,6 @@
     rows = queries.shape[2] // (heads * dim) * steps
     hbm = functools.partial(pltpu.with_memory_space_constraint, memory_space=pltpu.HBM)
     any_space = pl.BlockSpec(memory_space=pl.ANY)
-    smem = pl.BlockSpec(memory_space=pltpu.SMEM)
     vmem = pl.BlockSpec(memory_space=pltpu.VMEM)
     bf16, f32 = jnp.bfloat16, jnp.float32
     outs = (
@@ -287,19 +311,19 @@
         jax.ShapeDtypeStruct((per, 2, heads), bf16),
         jax.ShapeDtypeStruct((1,), f32),
     )
-    state = jax.ShapeDtypeStruct((per, heads, rows, dim), f32)
     results = pl.pallas_call(
         functools.partial(kernel, n),
         out_shape=(
             jax.ShapeDtypeStruct(queries.shape, bf16),
             jax.ShapeDtypeStruct((per,) + pool.shape[1:], bf16),
             jax.ShapeDtypeStruct((per, heads, rows, dim), bf16),
-            state, state, state,
+            jax.ShapeDtypeStruct((per, heads, rows, dim), f32),
             jax.ShapeDtypeStruct((per, 8, 128), f32),
+            outs[2],
             jax.ShapeDtypeStruct((8, 128), f32),
         ),
         in_specs=[any_space] * 7,
-        out_specs=(vmem,) * 8,
+        out_specs=(vmem,) * 7,
         scratch_shapes=[
             pltpu.VMEM(pool.shape, bf16),
             pltpu.VMEM(scale.shape[1:] + scale.shape[:1], bf16),
@@ -315,7 +339,7 @@
             pltpu.VMEM((slots, heads, rows, dim), f32),
             pltpu.VMEM((slots, heads, rows, dim), f32),
             pltpu.VMEM((slots, heads, rows, dim), f32),
-            pltpu.SemaphoreType.DMA,
+            pltpu.SemaphoreType.DMA((1,)),
             pltpu.SemaphoreType.DMA((6,)),
             pltpu.SemaphoreType.DMA((per, 2)),
             pltpu.SemaphoreType.DMA((per, 2)),
@@ -332,9 +356,15 @@
     return pl.pallas_call(
         functools.partial(merge_kernel, n),
         out_shape=outs,
-        in_specs=[vmem] * 8,
-        out_specs=(vmem, any_space, vmem, smem),
-        scratch_shapes=[pltpu.SemaphoreType.DMA((per,))],
+        in_specs=[vmem] * 7,
+        out_specs=(any_space,) * 4,
+        scratch_shapes=[
+            pltpu.VMEM(queries.shape, bf16),
+            pltpu.SMEM((1,), f32),
+            pltpu.SemaphoreType.DMA((per,)),
+            pltpu.SemaphoreType.DMA((2,)),
+            pltpu.SemaphoreType.DMA((heads,)),
+        ],
         compiler_params=pltpu.CompilerParams(vmem_limit_bytes=32 * 1024 * 1024),
     )(*results)
 

time: 20 us -> 15.9 us (0.80)
  the two profiles are of different devices: /device:TPU:0 before, /device:TPU:8 now
where the time goes in v3:
time: 15.9 us; the launch traced here: 15.8 us
  Pallas kernels  15.1 us (95%)
  between operations  0.64 us (4%)
    pallas_call x1, Pallas kernels, local(): pl.pallas_call(functools.partial(kernel, n), out_shape=(jax.ShapeDtypeStr...  14.2 us
    pallas_call x1, Pallas kernels, local(): pl.pallas_call(functools.partial(merge_kernel, n), out_shape=outs, in_spe...  0.9 us

profile of v3, /device:TPU:8, one launch (start us, length us, event | category | flops | bytes accessed | tf_op | source)
XLA Modules:
  0.0 15.8 jit_solution(15306481854377160683)
XLA Ops:
  0.6 14.2 %shard_map.102 = (bf16[8,4,2048]{2,1,0:T(4,128)(2,1)S(1)}, bf16[2,2,2,128,128]{4,3,2,1,0:T(8,128)(2,1)S(1)}, bf16[2,2,32,128]{3,2,1,0:T(8,128)(2,1)S(1)}, f32[2,...) custom-call(bf16[34,2,2,128,128]{4,3,2,1,0:T(8,128)(2,1)} %pool_hbm.1, ...), custom_call_target="tpu_custom_call" | custom-call | tf_op jit(solution)/shard_map/pallas_call | solution.py:314
  14.9 0.9 %shard_map.103 = (bf16[8,4,2048]{2,1,0:T(4,128)(2,1)}, bf16[2,2,2,128,128]{4,3,2,1,0:T(8,128)(2,1)}, bf16[2,2,2]{2,1,0:T(2,128)(2,1)}, f32[1]{0:T(128)}) custom-call(bf16[8,4,2048]{2,1,0:T(4,128)(2,1)S(1)} %get-tuple-element.11.att, bf16[2,2,2,128,128]{4,3,2,1,0:T(8,128)(2,1)S(1)} %get-tuple-element.12.arrived, ...), custom_call_target="tpu_custom_call" | custom-call | tf_op jit(solution)/shard_map/pallas_call | solution.py:356

commit v4 on v3

--- a/solution.py
+++ b/solution.py
@@ -21,35 +21,19 @@
 def kernel(
     n, pool_hbm, scale_hbm, lengths_hbm, table_hbm, moves_hbm, q_hbm, new_hbm,
     out_ref, arrived, p_out, acc_out, info_ref, arrival_ref, load_ref,
-    pool, scale, lengths, table, moves, q_ref, new_ref, staged, note, notes, qs, acc_s, m_s, l_s,
+    keys, values, scale, lengths, table, moves, q_ref, new_ref, staged, note, notes, qs, acc_s, m_s, l_s,
     pool_sem, in_sem, send_sem, recv_sem, note_send, note_recv,
 ):
     me = lax.axis_index("inst")
     slots, steps, _ = q_ref.shape
     per = staged.shape[0]
     blocks = table.shape[0]
-    heads, block_len, dim = pool.shape[2:]
+    heads, block_len, dim = keys.shape[1:]
     group = q_ref.shape[2] // (heads * dim)
     rows = group * steps
     width = group * dim
     scaling = 1.0 / math.sqrt(dim)
 
-    pieces = pool_sem.shape[0]
-    edges = [pool.shape[0] * i // pieces for i in range(pieces + 1)]
-    pool_copies = []
-    for i in range(pieces):
-        part = pl.ds(edges[i], edges[i + 1] - edges[i])
-        pool_copies.append(
-            pltpu.make_async_copy(pool_hbm.at[part], pool.at[part], pool_sem.at[i])
-        )
-    for copy in pool_copies:
-        copy.start()
-    barrier = pltpu.get_barrier_semaphore()
-    for k in range(1, n):
-        pl.semaphore_signal(
-            barrier, inc=1, device_id={"inst": lax.rem(me + k, n)},
-            device_id_type=pl.DeviceIdType.MESH,
-        )
     small = [
         pltpu.make_async_copy(x, y, in_sem.at[3 + i])
         for i, (x, y) in enumerate(
@@ -60,11 +44,23 @@
         copy.start()
     scale_copy = pltpu.make_async_copy(scale_hbm, scale, in_sem.at[0])
     scale_copy.start()
+    pool_copies = [
+        pltpu.make_async_copy(pool_hbm.at[:, kv], part, pool_sem.at[kv])
+        for kv, part in enumerate((keys, values))
+    ]
+    pool_copies[0].start()
+    pool_copies[1].start()
     q_copy = pltpu.make_async_copy(q_hbm, q_ref, in_sem.at[1])
     q_copy.start()
     new_copy = pltpu.make_async_copy(new_hbm, new_ref, in_sem.at[2])
     new_copy.start()
 
+    barrier = pltpu.get_barrier_semaphore()
+    for k in range(1, n):
+        pl.semaphore_signal(
+            barrier, inc=1, device_id={"inst": lax.rem(me + k, n)},
+            device_id_type=pl.DeviceIdType.MESH,
+        )
     for copy in small:
         copy.wait()
 
@@ -92,10 +88,9 @@
                 r = kv * heads + h
                 row = jnp.where(head_lane == h, pair[r : r + 1], row)
             note[j, pl.ds(kv, 1), :] = row
-    for copy in pool_copies:
-        copy.wait()
-    for j in range(per):
-        staged[j] = pool[moves[0, me * per + j]]
+    pool_copies[0].wait()
+    for j in range(per):
+        staged[j, 0] = keys[moves[0, me * per + j]]
     pl.semaphore_wait(barrier, n - 1)
 
     sends = []
@@ -119,14 +114,23 @@
                 device_id_type=pl.DeviceIdType.MESH,
             )
         )
-    for copy in note_sends + sends[:2]:
+    last = me == n - 1
+
+    def begin(kv):
+        sends[kv].start()
+
+        @pl.when(jnp.logical_not(last))
+        def _():
+            for j in range(1, per):
+                sends[2 * j + kv].start()
+
+    for copy in note_sends:
         copy.start()
-    last = me == n - 1
-
-    @pl.when(jnp.logical_not(last))
-    def _():
-        for copy in sends[2:]:
-            copy.start()
+    begin(0)
+    pool_copies[1].wait()
+    for j in range(per):
+        staged[j, 1] = values[moves[0, me * per + j]]
+    begin(1)
 
     sources = [lax.rem(me + n - 1 - j, n) for j in range(per)]
     arrival_rows = [sources[j] * per + j for j in range(per)]
@@ -147,7 +151,7 @@
         limit = jnp.where(hit, (count - 1) * block_len, length)
         q_all = q_ref[s].astype(jnp.float32)
         fresh = [new_ref[s, u].astype(jnp.float32) for u in range(steps)]
-        index = [jnp.clip(table[j, s], 0, pool.shape[0] - 1) for j in range(blocks)]
+        index = [jnp.clip(table[j, s], 0, keys.shape[0] - 1) for j in range(blocks)]
         scales = [block_scale(index[j]) for j in range(blocks)]
         pad = jnp.zeros((block_len - steps, dim), jnp.float32)
         for h in range(heads):
@@ -165,7 +169,7 @@
             scored = []
             for j in range(blocks):
                 raw = lax.dot_general(
-                    qh, pool[index[j], 0, h], TRANS, preferred_element_type=jnp.float32
+                    qh, keys[index[j], h], TRANS, preferred_element_type=jnp.float32
                 )
                 raw = raw * (scales[j][h : h + 1] * scaling)
                 scored.append(jnp.where(lane + j * block_len < limit, raw, NEG))
@@ -184,7 +188,7 @@
             for j in range(blocks):
                 w = (p[j] * scales[j][heads + h : heads + h + 1]).astype(jnp.bfloat16)
                 acc = acc + jnp.dot(
-                    w, pool[index[j], 1, h], preferred_element_type=jnp.float32
+                    w, values[index[j], h], preferred_element_type=jnp.float32
                 )
             acc_s[s, h] = acc
             m_s[s, h] = jnp.broadcast_to(top, (rows, dim))
@@ -325,7 +329,8 @@
         in_specs=[any_space] * 7,
         out_specs=(vmem,) * 7,
         scratch_shapes=[
-            pltpu.VMEM(pool.shape, bf16),
+            pltpu.VMEM(pool.shape[:1] + pool.shape[2:], bf16),
+            pltpu.VMEM(pool.shape[:1] + pool.shape[2:], bf16),
             pltpu.VMEM(scale.shape[1:] + scale.shape[:1], bf16),
             pltpu.SMEM(lengths.shape, jnp.int32),
             pltpu.SMEM(table.shape[::-1], jnp.int32),
@@ -339,7 +344,7 @@
             pltpu.VMEM((slots, heads, rows, dim), f32),
             pltpu.VMEM((slots, heads, rows, dim), f32),
             pltpu.VMEM((slots, heads, rows, dim), f32),
-            pltpu.SemaphoreType.DMA((1,)),
+            pltpu.SemaphoreType.DMA((2,)),
             pltpu.SemaphoreType.DMA((6,)),
             pltpu.SemaphoreType.DMA((per, 2)),
             pltpu.SemaphoreType.DMA((per, 2)),

time: 15.9 us -> 16 us (level)
  no operation moved by 1% of the time
where the time goes in v4:
time: 16 us; the launch traced here: 15.9 us
  Pallas kernels  15.2 us (95%)
  between operations  0.64 us (4%)
    pallas_call x1, Pallas kernels, local(): pl.pallas_call(functools.partial(kernel, n), out_shape=(jax.ShapeDtypeStr...  14.3 us
    pallas_call x1, Pallas kernels, local(): pl.pallas_call(functools.partial(merge_kernel, n), out_shape=outs, in_spe...  0.9 us

profile of v4, /device:TPU:8, one launch (start us, length us, event | category | flops | bytes accessed | tf_op | source)
XLA Modules:
  0.0 15.9 jit_solution(4240725830965314357)
XLA Ops:
  0.6 14.3 %shard_map.102 = (bf16[8,4,2048]{2,1,0:T(4,128)(2,1)S(1)}, bf16[2,2,2,128,128]{4,3,2,1,0:T(8,128)(2,1)S(1)}, bf16[2,2,32,128]{3,2,1,0:T(8,128)(2,1)S(1)}, f32[2,...) custom-call(bf16[34,2,2,128,128]{4,3,2,1,0:T(8,128)(2,1)} %pool_hbm.1, ...), custom_call_target="tpu_custom_call" | custom-call | tf_op jit(solution)/shard_map/pallas_call | solution.py:318
  15.0 0.9 %shard_map.103 = (bf16[8,4,2048]{2,1,0:T(4,128)(2,1)}, bf16[2,2,2,128,128]{4,3,2,1,0:T(8,128)(2,1)}, bf16[2,2,2]{2,1,0:T(2,128)(2,1)}, f32[1]{0:T(128)}) custom-call(bf16[8,4,2048]{2,1,0:T(4,128)(2,1)S(1)} %get-tuple-element.11.att, bf16[2,2,2,128,128]{4,3,2,1,0:T(8,128)(2,1)S(1)} %get-tuple-element.12.arrived, ...), custom_call_target="tpu_custom_call" | custom-call | tf_op jit(solution)/shard_map/pallas_call | solution.py:361
